TPU v7x, 32 devices: a whole 2x2x4 slice. The times are simulated.
32 devices in a mesh: row: 8 (over z, x), col: 2 (over y), rep: 2 (over core).
Axes of the slice: x: 2, y: 2, z: 4, core: 2. Of those that a mesh axis runs over, the one named last changes fastest.
Arguments:
- basis: bfloat16 [64, 1024, 128], P('row', None, 'rep'), may hold values from -6 to 6
- tiles: bfloat16 [8, 2, 4, 1024, 1024], P('row', 'col'), may hold values from -1.5 to 1.5
- slots: int32 [8, 2, 4, 2], P('row', 'col'), may hold values from -1 to 63, as said below
- sectors: int32 [64, 1024], replicated, may hold values from 0 to 10
Outputs:
- next_basis: float32 [64, 1024, 128], P('row', 'col', 'rep')
- projected: float32 [2, 128, 128], replicated
Inputs may be any that keep to these rules, and one draw needn't show every extreme that they name: For owner (r, c), the first two indices of slots, each live slot holds (I, J) with 8 * r <= I < 8 * (r + 1) and 32 * c <= J < 32 * (c + 1). Live slots come first, every owner has at least one, an empty slot holds (-1, -1). Each pair of block indices, in either order, is held by one live slot at most among all owners. At most 4 live slots an owner, and some owner has all 4 live.
All inputs are finite; a program needn't handle non-finite values.
Results may differ from a plain program's by a relative error of at most 0.0025.
Values may be sent and summed in bfloat16 or wider, within the bound.
A program may use at most 128 MiB of HBM per device.

v0:
```python
import jax
import jax.numpy as jnp
from jax import lax
from jax.sharding import PartitionSpec as P

PRODUCTS = 2


def projections(own_rows, previous, widened, rep_index, total_rows, full_cols):
    gram_block = jnp.dot(own_rows.T, widened, precision=lax.Precision.HIGHEST) / total_rows
    ritz_block = (
        jnp.dot(previous.astype(jnp.float32).T, widened, precision=lax.Precision.HIGHEST)
        / total_rows
    )
    zero_matrix = jnp.zeros((full_cols, full_cols), jnp.float32)
    row_start = rep_index * own_rows.shape[1]
    gram_part = lax.dynamic_update_slice_in_dim(zero_matrix, gram_block, row_start, 0)
    ritz_part = lax.dynamic_update_slice_in_dim(zero_matrix, ritz_block, row_start, 0)
    return (gram_part, ritz_part)


def solve_rows(gram_matrix, widened):
    factor = jnp.linalg.cholesky(gram_matrix)
    return jax.scipy.linalg.solve_triangular(factor, widened.T, lower=True).T


def body(basis, tiles, slots, sectors):
    row_count = lax.axis_size("row")
    col_count = lax.axis_size("col")
    row_index = lax.axis_index("row")
    col_index = lax.axis_index("col")
    rep_index = lax.axis_index("rep")
    blocks_here, tile_width, half_cols = basis.shape
    group_size = row_count // col_count
    col_blocks = blocks_here * group_size
    share_rows = tile_width // col_count
    total_rows = blocks_here * row_count * tile_width
    full_cols = half_cols * lax.axis_size("rep")
    slot_pairs = slots.reshape(-1, 2)
    tile_stack = tiles.reshape(-1, tile_width, tile_width)
    live_count = jnp.sum((slot_pairs[:, 0] >= 0).astype(jnp.int32))
    block_rows = jnp.maximum(slot_pairs[:, 0], 0)
    block_cols = jnp.maximum(slot_pairs[:, 1], 0)
    local_rows = jnp.clip(block_rows - blocks_here * row_index, 0, blocks_here - 1)
    local_cols = jnp.clip(block_cols - col_blocks * col_index, 0, col_blocks - 1)
    same_sector = sectors[block_rows][:, :, None] == sectors[block_cols][:, None, :]
    masked = jnp.where(same_sector, tile_stack, jnp.zeros((), tile_stack.dtype))
    row_panel = basis
    outcome = None
    history = []
    for rounds in range(PRODUCTS):
        whole_panel = lax.all_gather(row_panel, "row", axis=0, tiled=True)
        columns = lax.dynamic_slice_in_dim(whole_panel, col_index * col_blocks, col_blocks, 0)

        def accumulate(position, partials, columns=columns, row_panel=row_panel):
            row_totals, col_totals = partials
            one_tile = lax.dynamic_index_in_dim(masked, position, 0, keepdims=False)
            row_slot = local_rows[position]
            col_slot = local_cols[position]
            col_input = lax.dynamic_index_in_dim(columns, col_slot, 0, keepdims=False)
            row_input = lax.dynamic_index_in_dim(row_panel, row_slot, 0, keepdims=False)
            forward = jnp.dot(one_tile, col_input, preferred_element_type=jnp.float32)
            backward = lax.dot_general(
                one_tile, row_input, (((0,), (0,)), ((), ())), preferred_element_type=jnp.float32
            )
            return (row_totals.at[row_slot].add(forward), col_totals.at[col_slot].add(backward))

        initial = (jnp.zeros(row_panel.shape, jnp.float32), jnp.zeros(columns.shape, jnp.float32))
        row_part, col_part = lax.fori_loop(0, live_count, accumulate, initial)
        col_share = lax.psum_scatter(col_part, "row", scatter_dimension=1, tiled=True)
        col_total = lax.all_gather(col_share, "row", axis=1, tiled=True)
        own_block = lax.dynamic_slice_in_dim(
            col_total, row_index % group_size * blocks_here, blocks_here, 0
        )
        is_owner = row_index // group_size == col_index
        row_part = row_part + jnp.where(is_owner, own_block, jnp.zeros_like(own_block))
        summed = lax.psum(row_part, "col")
        own_rows = summed.reshape(-1, half_cols)
        previous = row_panel.reshape(-1, half_cols)
        widened = lax.all_gather(own_rows, "rep", axis=1, tiled=True)
        gram_part, ritz_part = projections(
            own_rows, previous, widened, rep_index, total_rows, full_cols
        )
        gram_matrix, ritz_matrix = lax.psum((gram_part, ritz_part), ("row", "rep"))
        solved = solve_rows(gram_matrix, widened)
        chosen = lax.dynamic_slice_in_dim(solved, rep_index * half_cols, half_cols, 1)
        next_block = chosen.reshape(blocks_here, tile_width, half_cols)
        outcome = lax.dynamic_slice_in_dim(next_block, col_index * share_rows, share_rows, 1)
        row_panel = lax.optimization_barrier(next_block.astype(jnp.bfloat16))
        history.append(ritz_matrix)
    return (outcome, jnp.stack(history))


def solution(mesh):
    placed = (
        P("row", None, "rep"),
        P("row", "col", None, None, None),
        P("row", "col", None, None),
        P(),
    )
    return jax.shard_map(
        body, mesh=mesh, in_specs=placed, out_specs=(P("row", "col", "rep"), P()), check_vma=False
    )
```

profile of v0, /device:TPU:0, one launch (start us, length us, event | category | flops | bytes accessed | tf_op | source)
XLA Modules:
  0.0 1371.9 jit_solution(6657256790378834700)
XLA Ops:
  10.6 7.8 compare_select_fusion
  18.4 119.4 %all-gather.7.cloned.1.call-done = bf16[64,1024,64]{1,2,0:T(8,128)(2,1)} async-done(((bf16[8,1024,64]{1,2,0:T(8,128)(2,1)}), bf16[64,1024,64]{1,2,0:T(8,128)(2,1)}) %all-gather.7.cloned.1.call-update) | async-done | bytes 8388624 | tf_op jit(solution)/shard_map/all_gather | solution.py:52
  137.8 4.8 constant_dynamic-slice_fusion.4
  142.9 4.3 broadcast.149.clone
  147.2 13.8 %while.28 = (s32[]{:T(128)}, f32[8,1024,64]{1,2,0:T(8,128)S(1)}, f32[32,1024,64]{1,2,0:T(8,128)}, s32[]{:T(128)}, s32[4]{0:T(128)S(1)}, /*index=5*/bf16[4,1024,1...) while((s32[]{:T(128)}, f32[8,1024,64]{1,2,0:T(8,128)S(1)}, ...), condition=%wide.region_4.5_spmd, body=%wide.region_1.4_spmd.sunk | while | flops 268697664 | bytes 5508433 | solution.py:69
  156.8 3.5 fusion.113
  161.1 186.9 %reduce-scatter.3.cloned.1.call-done = f32[32,128,64]{1,2,0:T(8,128)} async-done(((f32[32,1024,64]{1,2,0:T(8,128)}), f32[32,128,64]{1,2,0:T(8,128)}) %reduce-scatter.3.cloned.1.call-update) | async-done | bytes 1048592 | tf_op jit(solution)/shard_map/reduce_scatter | solution.py:70
  348.0 126.6 %all-gather.9.cloned.1.call-done = f32[32,1024,64]{1,2,0:T(8,128)} async-done(((f32[32,128,64]{1,2,0:T(8,128)}), f32[32,1024,64]{1,2,0:T(8,128)}) %all-gather.9.cloned.1.call-update) | async-done | bytes 8388624 | tf_op jit(solution)/shard_map/all_gather | solution.py:71
  478.2 61.2 %all-reduce.6.cloned.1.call-done = f32[8192,64]{0,1:T(8,128)} async-done(((f32[8192,64]{0,1:T(8,128)}), f32[8192,64]{0,1:T(8,128)}) %all-reduce.6.cloned.1.call-update) | async-done | bytes 2097168 | tf_op jit(solution)/shard_map/psum | solution.py:77
  539.5 15.0 %all-gather.11.cloned.1.call-done = f32[8192,128]{0,1:T(8,128)} async-done(((f32[8192,64]{0,1:T(8,128)}), f32[8192,128]{0,1:T(8,128)}) %all-gather.11.cloned.1.call-update) | async-done | bytes 4194320 | tf_op jit(solution)/shard_map/all_gather | solution.py:80
  554.5 5.9 convolution_multiply_fusion.2
  562.0 85.4 %all-reduce.8.cloned.1.call-done = f32[128,128]{0,1:T(8,128)} async-done(((f32[128,128]{0,1:T(8,128)}), f32[128,128]{0,1:T(8,128)}) %all-reduce.8.cloned.1.call-update) | async-done | bytes 65552 | tf_op jit(solution)/shard_map/psum | solution.py:84
  649.2 11.7 cholesky.44
  662.2 9.8 custom-call.6
  672.1 6.0 fusion.73
  680.6 126.5 %all-gather.13.cloned.1.call-done = bf16[64,1024,64]{1,2,0:T(8,128)(2,1)} async-done(((bf16[8,1024,64]{1,2,0:T(8,128)(2,1)}), bf16[64,1024,64]{1,2,0:T(8,128)(2,1)}) %all-gather.13.cloned.1.call-update) | async-done | bytes 8388624 | tf_op jit(solution)/shard_map/all_gather | solution.py:52
  807.0 4.9 constant_dynamic-slice_fusion.3
  812.2 4.3 broadcast.149
  816.5 14.8 %while.29 = (s32[]{:T(128)}, f32[8,1024,64]{1,2,0:T(8,128)S(1)}, f32[32,1024,64]{1,2,0:T(8,128)}, s32[]{:T(128)}, s32[4]{0:T(128)S(1)}, /*index=5*/bf16[4,1024,1...) while((s32[]{:T(128)}, f32[8,1024,64]{1,2,0:T(8,128)S(1)}, ...), condition=%wide.region_13.16_spmd, body=%wide.region_10.15_spmd.sunk | while | flops 268697664 | bytes 6163285 | solution.py:69
  824.1 2.9 fusion.118
  827.0 3.5 fusion.119
  831.3 189.9 %reduce-scatter.5.cloned.1.call-done = f32[32,128,64]{1,2,0:T(8,128)} async-done(((f32[32,1024,64]{1,2,0:T(8,128)}), f32[32,128,64]{1,2,0:T(8,128)}) %reduce-scatter.5.cloned.1.call-update) | async-done | bytes 1048592 | tf_op jit(solution)/shard_map/reduce_scatter | solution.py:70
  1021.3 126.4 %all-gather.15.cloned.1.call-done = f32[32,1024,64]{1,2,0:T(8,128)} async-done(((f32[32,128,64]{1,2,0:T(8,128)}), f32[32,1024,64]{1,2,0:T(8,128)}) %all-gather.15.cloned.1.call-update) | async-done | bytes 8388624 | tf_op jit(solution)/shard_map/all_gather | solution.py:71
  1151.3 61.2 %all-reduce.10.cloned.1.call-done = f32[8192,64]{0,1:T(8,128)} async-done(((f32[8192,64]{0,1:T(8,128)}), f32[8192,64]{0,1:T(8,128)}) %all-reduce.10.cloned.1.call-update) | async-done | bytes 2097168 | tf_op jit(solution)/shard_map/psum | solution.py:77
  1212.7 4.7 fusion.77
  1219.0 8.8 all-gather.17.cloned.1.call-done
  1227.8 4.5 fusion.75
  1232.4 5.5 convolution_multiply_fusion.1
  1239.0 91.9 %all-reduce.12.cloned.1.call-done = (f32[128,128]{0,1:T(8,128)}, f32[1,128,128]{2,1,0:T(8,128)}, f32[1,128,128]{2,1,0:T(8,128)}) async-done(((f32[128,128]{0,1:T(8,128)}, f32[1,128,128]{2,1,0:T(8,128)}, f32[1,128,128]{2,1,0:T(8,128)}), (f32[128,128]{0,1:T(8,128)}, f32[1,128,128]{2,1,0:T(8,128)}, f32[1,128,128]{2,1,0:T(8,128)})) %all-reduce.12.cloned.1.call-update) | async-done | bytes 196624 | tf_op jit(solution)/shard_map/psum | solution.py:84
  1332.7 11.7 cholesky.55
  1345.8 9.8 custom-call.7
  1355.6 5.5 fusion.71
  (95 shorter events, 36.1 us)
Async XLA Ops:
  7.2 2.3 copy-start
  7.2 130.6 %all-gather.7.cloned.1.call-start = ((), (), s32[]{:S(2)}) async-start(), calls=%async_computation.2 | async-start | bytes 9437184 | tf_op jit(solution)/shard_map/all_gather | solution.py:52
  7.9 340.0 %reduce-scatter.3.cloned.1.call-start = ((), (), s32[]{:S(2)}) async-start(), calls=%async_computation.3 | async-start | bytes 9437184 | tf_op jit(solution)/shard_map/reduce_scatter | solution.py:70
  142.9 4.3 copy-start.10
  142.9 4.3 copy-start.11
  161.0 313.6 %all-gather.9.cloned.1.call-start = ((), (), s32[]{:S(2)}) async-start(), calls=%async_computation.4 | async-start | bytes 9437184 | tf_op jit(solution)/shard_map/all_gather | solution.py:71
  348.0 191.4 %all-reduce.6.cloned.1.call-start = ((), (), s32[]{:S(2)}) async-start(), calls=%async_computation.5 | async-start | bytes 4194304 | tf_op jit(solution)/shard_map/psum | solution.py:77
  478.1 76.4 %all-gather.11.cloned.1.call-start = ((), (), s32[]{:S(2)}) async-start(), calls=%async_computation.6 | async-start | bytes 6291456 | tf_op jit(solution)/shard_map/all_gather | solution.py:80
  539.4 108.0 %all-reduce.8.cloned.1.call-start = ((), (), s32[]{:S(2)}) async-start(), calls=%async_computation.7 | async-start | bytes 131072 | tf_op jit(solution)/shard_map/psum | solution.py:84
  560.8 0.6 copy-start.7
  561.5 245.6 %all-gather.13.cloned.1.call-start = ((), (), s32[]{:S(2)}) async-start(), calls=%async_computation.8 | async-start | bytes 9437184 | tf_op jit(solution)/shard_map/all_gather | solution.py:52
  680.4 340.9 %reduce-scatter.5.cloned.1.call-start = ((), (), s32[]{:S(2)}) async-start(), calls=%async_computation.9 | async-start | bytes 9437184 | tf_op jit(solution)/shard_map/reduce_scatter | solution.py:70
  831.3 316.4 %all-gather.15.cloned.1.call-start = ((), (), s32[]{:S(2)}) async-start(), calls=%async_computation.10 | async-start | bytes 9437184 | tf_op jit(solution)/shard_map/all_gather | solution.py:71
  1021.2 191.2 %all-reduce.10.cloned.1.call-start = ((), (), s32[]{:S(2)}) async-start(), calls=%async_computation.11 | async-start | bytes 4194304 | tf_op jit(solution)/shard_map/psum | solution.py:77
  1149.7 62.8 %copy-start.3 = (bf16[8,1024,64]{1,2,0:T(8,128)(2,1)S(1)}, bf16[8,1024,64]{1,2,0:T(8,128)(2,1)}, u32[]{:S(2)}) copy-start(bf16[8,1024,64]{1,2,0:T(8,128)(2,1)} %get-tuple-element.499) | copy-start | bytes 3145732
  1151.2 76.6 %all-gather.17.cloned.1.call-start = ((), (), s32[]{:S(2)}) async-start(), calls=%async_computation.12 | async-start | bytes 6291456 | tf_op jit(solution)/shard_map/all_gather | solution.py:80
  1212.5 118.4 %all-reduce.12.cloned.1.call-start = ((), (), s32[]{:S(2)}) async-start(), calls=%async_computation.13 | async-start | bytes 393216 | tf_op jit(solution)/shard_map/psum | solution.py:84
  1217.4 20.5 %copy-start.4 = (f32[1,128,128]{2,1,0:T(8,128)}, f32[1,128,128]{2,1,0:T(8,128)S(1)}, u32[]{:S(2)}) copy-start(f32[1,128,128]{2,1,0:T(8,128)S(1)} %fusion.77) | copy-start | bytes 196612
  1217.4 15.0 %copy-start.2 = (f32[8192,64]{0,1:T(8,128)S(1)}, f32[8192,64]{0,1:T(8,128)}, u32[]{:S(2)}) copy-start(f32[8192,64]{0,1:T(8,128)} %all-reduce.10.cloned.1.call-done) | copy-start | bytes 6291460
  1238.3 0.6 copy-start.6
  1238.4 0.6 copy-start.5
  1361.2 3.7 copy-start.1
  1361.2 3.0 copy-start.8
  1361.2 3.0 copy-start.9
Sparse Core Ops, SparseCore 0:
  10.1 127.6 all-gather.6
  161.2 186.7 reduce-scatter.2
  350.2 124.3 all-gather.8
  478.2 61.0 all-reduce.5
  540.8 13.6 all-gather.10
  561.6 85.7 all-reduce.7
  680.5 126.5 all-gather.12
  831.4 189.7 reduce-scatter.4
  1023.3 124.3 all-gather.14
  1151.3 61.0 all-reduce.9
  1214.1 13.6 all-gather.16
  1239.1 91.7 all-reduce.11
where the time goes:
time: 1380 us; the launch traced here: 1370 us
  waiting for transfers between devices  1200 us (87%)
  other arithmetic  62.9 us (5%)
  matrix products  44.9 us (3%)
  local copies, waits for them, and re-layouts  37.5 us (3%)
  between operations  14.8 us (1%)
    reduce_scatter x2, waiting for transfers between devices, body(): lax.psum_scatter(col_part, 'row', scatter_dimension=1, tiled=True)  377 us
    all_gather x2, waiting for transfers between devices, body(): col_total = lax.all_gather(col_share, 'row', axis=1, tiled=True)  253 us
    all_gather x2, waiting for transfers between devices, body(): whole_panel = lax.all_gather(row_panel, 'row', axis=0, tiled=True)  246 us
    psum x2, waiting for transfers between devices, body(): gram_matrix, ritz_matrix = lax.psum((gram_part, ritz_part), ('row', 'rep'))  177 us
    psum x2, waiting for transfers between devices, body(): summed = lax.psum(row_part, 'col')  122 us
  transfers between devices with their start and end apart: 12, of which 12 were waited for; matrix products, arithmetic and copies ran while one was open for 1% of the time, Pallas kernels for 0%

commit v1 on v0

--- a/solution.py
+++ b/solution.py
@@ -68,7 +68,15 @@
         initial = (jnp.zeros(row_panel.shape, jnp.float32), jnp.zeros(columns.shape, jnp.float32))
         row_part, col_part = lax.fori_loop(0, live_count, accumulate, initial)
         col_share = lax.psum_scatter(col_part, "row", scatter_dimension=1, tiled=True)
-        col_total = lax.all_gather(col_share, "row", axis=1, tiled=True)
+        ways, here = (lax.axis_size("row"), lax.axis_index("row"))
+        grown, reach = (col_share, 1)
+        while reach < ways:
+            theirs = lax.ppermute(grown, "row", [(d, d ^ reach) for d in range(ways)])
+            mine_first = jnp.concatenate([grown, theirs], axis=1)
+            theirs_first = jnp.concatenate([theirs, grown], axis=1)
+            grown = jnp.where(here & reach == 0, mine_first, theirs_first)
+            reach = 2 * reach
+        col_total = grown
         own_block = lax.dynamic_slice_in_dim(
             col_total, row_index % group_size * blocks_here, blocks_here, 0
         )

time: 1380 us -> 1650 us (1.20)
  waiting for transfers between devices: 1200 us -> 1450 us
    ppermute x0 -> x6, waiting for transfers between devices: none -> 501 us  [body(): theirs = lax.ppermute(grown, 'row', [(d, d ^ reach) for d in range(ways)])]
    all_gather x2 -> x0, waiting for transfers between devices: 253 us -> none  [body(): col_total = lax.all_gather(col_share, 'row', axis=1, tiled=True)]
  transfers between devices with their start and end apart: 12 -> 16, of which waited for: 12 -> 16; matrix products, arithmetic and copies ran while one was open for 1% -> 1% of each run, Pallas kernels for 0% -> 0%
where the time goes in v1:
time: 1650 us; the launch traced here: 1640 us
  waiting for transfers between devices  1450 us (88%)
  other arithmetic  74.7 us (5%)
  matrix products  44.9 us (3%)
  local copies, waits for them, and re-layouts  37.7 us (2%)
    ppermute x6, waiting for transfers between devices, body(): theirs = lax.ppermute(grown, 'row', [(d, d ^ reach) for d in range(ways)])  501 us
    reduce_scatter x2, waiting for transfers between devices, body(): lax.psum_scatter(col_part, 'row', scatter_dimension=1, tiled=True)  377 us
    all_gather x2, waiting for transfers between devices, body(): whole_panel = lax.all_gather(row_panel, 'row', axis=0, tiled=True)  246 us
    psum x2, waiting for transfers between devices, body(): gram_matrix, ritz_matrix = lax.psum((gram_part, ritz_part), ('row', 'rep'))  177 us
    psum x2, waiting for transfers between devices, body(): summed = lax.psum(row_part, 'col')  125 us
  transfers between devices with their start and end apart: 16, of which 16 were waited for; matrix products, arithmetic and copies ran while one was open for 1% of the time, Pallas kernels for 0%

profile of v1, /device:TPU:0, one launch (start us, length us, event | category | flops | bytes accessed | tf_op | source)
XLA Modules:
  0.0 1640.7 jit_solution(95200692921155857)
XLA Ops:
  10.6 7.8 compare_select_fusion
  18.4 119.4 %all-gather.5.cloned.1.call-done = bf16[64,1024,64]{1,2,0:T(8,128)(2,1)} async-done(((bf16[8,1024,64]{1,2,0:T(8,128)(2,1)}), bf16[64,1024,64]{1,2,0:T(8,128)(2,1)}) %all-gather.5.cloned.1.call-update) | async-done | bytes 8388624 | tf_op jit(solution)/shard_map/all_gather | solution.py:52
  137.8 4.8 constant_dynamic-slice_fusion.4
  147.2 13.8 while.28
  161.1 186.9 %reduce-scatter.3.cloned.1.call-done = f32[32,128,64]{1,2,0:T(8,128)} async-done(((f32[32,1024,64]{1,2,0:T(8,128)}), f32[32,128,64]{1,2,0:T(8,128)}) %reduce-scatter.3.cloned.1.call-update) | async-done | bytes 1048592 | tf_op jit(solution)/shard_map/reduce_scatter | solution.py:70
  349.4 23.7 %collective-permute-done = f32[32,128,64]{1,2,0:T(8,128)S(1)} collective-permute-done((f32[32,128,64]{1,2,0:T(8,128)}, f32[32,128,64]{1,2,0:T(8,128)S(1)}, u32[]{:S(2)}, u32[]{:S(2)}) %collective-permute-start) | collective-permute-done | bytes 1048608 | tf_op jit(solution)/shard_map/ppermute | solution.py:74
  376.3 46.9 %collective-permute-done.1 = f32[32,256,64]{1,2,0:T(8,128)} collective-permute-done((f32[32,256,64]{1,2,0:T(8,128)}, f32[32,256,64]{1,2,0:T(8,128)}, u32[]{:S(2)}, u32[]{:S(2)}) %collective-permute-start.1) | collective-permute-done | bytes 2097184 | tf_op jit(solution)/shard_map/ppermute | solution.py:74
  423.2 6.5 maximum_select_fusion
  430.9 180.5 %collective-permute-done.2 = f32[32,512,64]{1,2,0:T(8,128)} collective-permute-done((f32[32,512,64]{1,2,0:T(8,128)}, f32[32,512,64]{1,2,0:T(8,128)}, u32[]{:S(2)}, u32[]{:S(2)}) %collective-permute-start.2) | collective-permute-done | bytes 4194336 | tf_op jit(solution)/shard_map/ppermute | solution.py:74
  615.9 62.7 %all-reduce.6.cloned.1.call-done = f32[8192,64]{0,1:T(8,128)} async-done(((f32[8192,64]{0,1:T(8,128)}), f32[8192,64]{0,1:T(8,128)}) %all-reduce.6.cloned.1.call-update) | async-done | bytes 2097168 | tf_op jit(solution)/shard_map/psum | solution.py:85
  678.7 15.0 all-gather.7.cloned.1.call-done
  693.7 5.9 convolution_multiply_fusion.2
  701.2 85.4 %all-reduce.8.cloned.1.call-done = f32[128,128]{0,1:T(8,128)} async-done(((f32[128,128]{0,1:T(8,128)}), f32[128,128]{0,1:T(8,128)}) %all-reduce.8.cloned.1.call-update) | async-done | bytes 65552 | tf_op jit(solution)/shard_map/psum | solution.py:92
  788.4 11.7 cholesky.44
  801.5 9.8 custom-call.6
  811.3 6.0 fusion.73
  819.8 126.5 %all-gather.9.cloned.1.call-done = bf16[64,1024,64]{1,2,0:T(8,128)(2,1)} async-done(((bf16[8,1024,64]{1,2,0:T(8,128)(2,1)}), bf16[64,1024,64]{1,2,0:T(8,128)(2,1)}) %all-gather.9.cloned.1.call-update) | async-done | bytes 8388624 | tf_op jit(solution)/shard_map/all_gather | solution.py:52
  946.3 4.9 constant_dynamic-slice_fusion.3
  955.7 14.8 while.29
  970.5 189.9 %reduce-scatter.5.cloned.1.call-done = f32[32,128,64]{1,2,0:T(8,128)} async-done(((f32[32,1024,64]{1,2,0:T(8,128)}), f32[32,128,64]{1,2,0:T(8,128)}) %reduce-scatter.5.cloned.1.call-update) | async-done | bytes 1048592 | tf_op jit(solution)/shard_map/reduce_scatter | solution.py:70
  1161.9 23.7 %collective-permute-done.3 = f32[32,128,64]{1,2,0:T(8,128)S(1)} collective-permute-done((f32[32,128,64]{1,2,0:T(8,128)}, f32[32,128,64]{1,2,0:T(8,128)S(1)}, u32[]{:S(2)}, u32[]{:S(2)}) %collective-permute-start.3) | collective-permute-done | bytes 1048608 | tf_op jit(solution)/shard_map/ppermute | solution.py:74
  1187.5 46.6 %collective-permute-done.4 = f32[32,256,64]{1,2,0:T(8,128)S(1)} collective-permute-done((f32[32,256,64]{1,2,0:T(8,128)S(1)}, f32[32,256,64]{1,2,0:T(8,128)S(1)}, u32[]{:S(2)}, u32[]{:S(2)}) %collective-permute-start.4) | collective-permute-done | bytes 2097184 | tf_op jit(solution)/shard_map/ppermute | solution.py:74
  1236.2 180.1 %collective-permute-done.5 = f32[32,512,64]{1,2,0:T(8,128)S(1)} collective-permute-done((f32[32,512,64]{1,2,0:T(8,128)S(1)}, f32[32,512,64]{1,2,0:T(8,128)S(1)}, u32[]{:S(2)}, u32[]{:S(2)}) %collective-permute-start.5) | collective-permute-done | bytes 4194336 | tf_op jit(solution)/shard_map/ppermute | solution.py:74
  1418.7 62.6 %all-reduce.10.cloned.1.call-done = f32[8192,64]{0,1:T(8,128)} async-done(((f32[8192,64]{0,1:T(8,128)}), f32[8192,64]{0,1:T(8,128)}) %all-reduce.10.cloned.1.call-update) | async-done | bytes 2097168 | tf_op jit(solution)/shard_map/psum | solution.py:85
  1481.5 4.8 fusion.89
  1487.8 8.8 all-gather.11.cloned.1.call-done
  1496.7 4.5 fusion.87
  1501.2 5.5 convolution_multiply_fusion.1
  1507.9 91.9 %all-reduce.12.cloned.1.call-done = (f32[128,128]{0,1:T(8,128)}, f32[1,128,128]{2,1,0:T(8,128)}, f32[1,128,128]{2,1,0:T(8,128)}) async-done(((f32[128,128]{0,1:T(8,128)}, f32[1,128,128]{2,1,0:T(8,128)}, f32[1,128,128]{2,1,0:T(8,128)}), (f32[128,128]{0,1:T(8,128)}, f32[1,128,128]{2,1,0:T(8,128)}, f32[1,128,128]{2,1,0:T(8,128)})) %all-reduce.12.cloned.1.call-update) | async-done | bytes 196624 | tf_op jit(solution)/shard_map/psum | solution.py:92
  1601.5 11.7 cholesky.55
  1614.6 9.8 custom-call.7
  1624.4 5.5 fusion.71
  (105 shorter events, 65.6 us)
Async XLA Ops:
  7.2 2.3 copy-start
  7.2 130.6 %all-gather.5.cloned.1.call-start = ((), (), s32[]{:S(2)}) async-start(), calls=%async_computation.2 | async-start | bytes 9437184 | tf_op jit(solution)/shard_map/all_gather | solution.py:52
  7.9 340.0 %reduce-scatter.3.cloned.1.call-start = ((), (), s32[]{:S(2)}) async-start(), calls=%async_computation.3 | async-start | bytes 9437184 | tf_op jit(solution)/shard_map/reduce_scatter | solution.py:70
  142.9 4.3 copy-start.10
  142.9 4.3 copy-start.11
  161.0 517.6 %all-reduce.6.cloned.1.call-start = ((), (), s32[]{:S(2)}) async-start(), calls=%async_computation.4 | async-start | bytes 4194304 | tf_op jit(solution)/shard_map/psum | solution.py:85
  347.9 25.2 %collective-permute-start = (f32[32,128,64]{1,2,0:T(8,128)}, f32[32,128,64]{1,2,0:T(8,128)S(1)}, u32[]{:S(2)}, u32[]{:S(2)}) collective-permute-start(f32[32,128,64]{1,2,0:T(8,128)} %reduce-scatter.3.cloned.1.call-done), channel_id=1, source_target_pairs={{0,4},{4,0},{8,12},{12,8},{16,20},{20,16},{24,28},{28,24},{1,5},{5... | collective-permute-start | bytes 3145736 | tf_op jit(solution)/shard_map/ppermute | solution.py:74
  376.3 46.9 %collective-permute-start.1 = (f32[32,256,64]{1,2,0:T(8,128)}, f32[32,256,64]{1,2,0:T(8,128)}, u32[]{:S(2)}, u32[]{:S(2)}) collective-permute-start(f32[32,256,64]{1,2,0:T(8,128)} %maximum_select_fusion.2), channel_id=1, source_target_pairs={{0,8},{4,12},{8,0},{12,4},{16,24},{20,28},{24,16},{28,20},{1,9},{5... | collective-permute-start | bytes 6291464 | tf_op jit(solution)/shard_map/ppermute | solution.py:74
  429.7 181.7 %collective-permute-start.2 = (f32[32,512,64]{1,2,0:T(8,128)}, f32[32,512,64]{1,2,0:T(8,128)}, u32[]{:S(2)}, u32[]{:S(2)}) collective-permute-start(f32[32,512,64]{1,2,0:T(8,128)} %maximum_select_fusion), channel_id=1, source_target_pairs={{0,16},{4,20},{8,24},{12,28},{16,0},{20,4},{24,8},{28,12},{1,17},{... | collective-permute-start | bytes 12582920 | tf_op jit(solution)/shard_map/ppermute | solution.py:74
  615.8 77.9 %all-gather.7.cloned.1.call-start = ((), (), s32[]{:S(2)}) async-start(), calls=%async_computation.5 | async-start | bytes 6291456 | tf_op jit(solution)/shard_map/all_gather | solution.py:88
  678.6 108.0 %all-reduce.8.cloned.1.call-start = ((), (), s32[]{:S(2)}) async-start(), calls=%async_computation.6 | async-start | bytes 131072 | tf_op jit(solution)/shard_map/psum | solution.py:92
  700.0 0.6 copy-start.7
  700.7 245.6 %all-gather.9.cloned.1.call-start = ((), (), s32[]{:S(2)}) async-start(), calls=%async_computation.7 | async-start | bytes 9437184 | tf_op jit(solution)/shard_map/all_gather | solution.py:52
  819.6 340.9 %reduce-scatter.5.cloned.1.call-start = ((), (), s32[]{:S(2)}) async-start(), calls=%async_computation.8 | async-start | bytes 9437184 | tf_op jit(solution)/shard_map/reduce_scatter | solution.py:70
  970.5 510.8 %all-reduce.10.cloned.1.call-start = ((), (), s32[]{:S(2)}) async-start(), calls=%async_computation.9 | async-start | bytes 4194304 | tf_op jit(solution)/shard_map/psum | solution.py:85
  1160.4 25.2 %collective-permute-start.3 = (f32[32,128,64]{1,2,0:T(8,128)}, f32[32,128,64]{1,2,0:T(8,128)S(1)}, u32[]{:S(2)}, u32[]{:S(2)}) collective-permute-start(f32[32,128,64]{1,2,0:T(8,128)} %reduce-scatter.5.cloned.1.call-done), channel_id=1, source_target_pairs={{0,4},{4,0},{8,12},{12,8},{16,20},{20,16},{24,28},{28,24},{1,5},{5... | collective-permute-start | bytes 3145736 | tf_op jit(solution)/shard_map/ppermute | solution.py:74
  1187.5 46.6 %collective-permute-start.4 = (f32[32,256,64]{1,2,0:T(8,128)S(1)}, f32[32,256,64]{1,2,0:T(8,128)S(1)}, u32[]{:S(2)}, u32[]{:S(2)}) collective-permute-start(f32[32,256,64]{1,2,0:T(8,128)S(1)} %maximum_select_fusion.3), channel_id=1, source_target_pairs={{0,8},{4,12},{8,0},{12,4},{16,24},{20,28},{24,16},{28,20},{1,9},{5... | collective-permute-start | bytes 6291464 | tf_op jit(solution)/shard_map/ppermute | solution.py:74
  1234.9 181.4 %collective-permute-start.5 = (f32[32,512,64]{1,2,0:T(8,128)S(1)}, f32[32,512,64]{1,2,0:T(8,128)S(1)}, u32[]{:S(2)}, u32[]{:S(2)}) collective-permute-start(f32[32,512,64]{1,2,0:T(8,128)S(1)} %maximum_select_fusion.1), channel_id=1, source_target_pairs={{0,16},{4,20},{8,24},{12,28},{16,0},{20,4},{24,8},{28,12},{1,17},{... | collective-permute-start | bytes 12582920 | tf_op jit(solution)/shard_map/ppermute | solution.py:74
  1417.0 64.4 %copy-start.3 = (bf16[8,1024,64]{1,2,0:T(8,128)(2,1)S(1)}, bf16[8,1024,64]{1,2,0:T(8,128)(2,1)}, u32[]{:S(2)}) copy-start(bf16[8,1024,64]{1,2,0:T(8,128)(2,1)} %get-tuple-element.499) | copy-start | bytes 3145732
  1418.7 78.0 %all-gather.11.cloned.1.call-start = ((), (), s32[]{:S(2)}) async-start(), calls=%async_computation.10 | async-start | bytes 6291456 | tf_op jit(solution)/shard_map/all_gather | solution.py:88
  1481.3 118.4 %all-reduce.12.cloned.1.call-start = ((), (), s32[]{:S(2)}) async-start(), calls=%async_computation.11 | async-start | bytes 393216 | tf_op jit(solution)/shard_map/psum | solution.py:92
  1486.2 20.5 %copy-start.4 = (f32[1,128,128]{2,1,0:T(8,128)}, f32[1,128,128]{2,1,0:T(8,128)S(1)}, u32[]{:S(2)}) copy-start(f32[1,128,128]{2,1,0:T(8,128)S(1)} %fusion.89) | copy-start | bytes 196612
  1486.3 15.0 copy-start.2
  1507.2 0.6 copy-start.6
  1507.2 0.6 copy-start.5
  1630.0 3.7 copy-start.1
  1630.0 3.0 copy-start.8
  1630.0 3.0 copy-start.9
Sparse Core Ops, SparseCore 0:
  10.1 127.6 all-gather.4
  161.2 186.7 reduce-scatter.2
  616.0 62.5 all-reduce.5
  680.0 13.6 all-gather.6
  700.8 85.7 all-reduce.7
  819.7 126.5 all-gather.8
  970.6 189.7 reduce-scatter.4
  1418.8 62.4 all-reduce.9
  1482.9 13.6 all-gather.10
  1508.0 91.6 all-reduce.11
